TPU v7x, 128 devices: a whole 4x4x4 slice. The times are simulated.
128 devices in a mesh: files: 16 (over z, y), clus: 8 (over x, core).
Axes of the slice: x: 4, y: 4, z: 4, core: 2. Of those that a mesh axis runs over, the one named last changes fastest.
Arguments:
- embeddings: bfloat16 [131072, 512], P(('files', 'clus')), may hold values from -192 to 192
- cluster_ids: int32 [131072, 1], P(('files', 'clus')), may hold values from 0 to 63; in each aligned block of 1024 rows (0 to 1023, 1024 to 2047, ...) at most 32 rows name the same one
Outputs:
- earlier_best: float32 [131072], P(('files', 'clus'))
- later_best: float32 [131072], P(('files', 'clus'))
Inputs may be any that keep to these rules, and one draw needn't show every extreme that they name: `cluster_ids`: within the rows of one device (aligned blocks of 1024 rows) no cluster is named by more than 32 rows, a bound that some block reaches.
All inputs are finite; a program needn't handle non-finite values.
Results may differ from a plain program's by a relative error of at most 0.00084.
Values may be sent and summed in bfloat16 or wider, within the bound.
A program may use at most 64 MiB of HBM per device.

v0:
```python
import jax
import jax.numpy as jnp
from jax import lax
from jax.sharding import PartitionSpec as P

CPF = 4
CAP = 32


def tile_maxima(own, own_ids, other, other_ids):
    similar = jnp.einsum("qmd,qnd->qmn", own, other, preferred_element_type=jnp.float32)
    mine = own_ids[:, :, None]
    theirs = other_ids[:, None, :]
    before = (theirs >= 0) & (theirs < mine)
    after = theirs > mine
    floor_value = jnp.float32(-1.0)
    row_first = jnp.max(jnp.where(before, similar, floor_value), axis=2)
    row_second = jnp.max(jnp.where(after, similar, floor_value), axis=2)
    return (similar, row_first, row_second)


def body(embeddings, cluster_ids):
    rows_here = embeddings.shape[0]
    width = embeddings.shape[1]
    group = lax.axis_size("clus")
    devices = lax.axis_size(("files", "clus"))
    per_owner = CPF
    clusters = per_owner * lax.axis_size("files")
    slots = CAP // group
    e = embeddings.astype(jnp.float32)
    squares = jnp.sum(e * e, axis=1, keepdims=True) + 1e-06
    unit = (e * lax.rsqrt(squares)).astype(jnp.bfloat16)
    labels = cluster_ids[:, 0]
    global_ids = lax.axis_index(("files", "clus")) * rows_here + jnp.arange(
        rows_here, dtype=jnp.int32
    )
    onehot = (labels[:, None] == jnp.arange(clusters, dtype=jnp.int32)[None, :]).astype(jnp.int32)
    rank = jnp.sum((jnp.cumsum(onehot, axis=0) - onehot) * onehot, axis=1)
    target = labels // per_owner * group + rank % group
    flat = (target * per_owner + labels % per_owner) * slots + rank // group
    outgoing = jnp.zeros((devices * per_owner * slots, width), jnp.bfloat16).at[flat].set(unit)
    outgoing_ids = jnp.full((devices * per_owner * slots,), -1, jnp.int32).at[flat].set(global_ids)
    outgoing = outgoing.reshape(devices, per_owner, slots, width)
    outgoing_ids = outgoing_ids.reshape(devices, per_owner, slots)
    blocks, block_ids = (
        lax.all_to_all(outgoing, ("files", "clus"), split_axis=0, concat_axis=2, tiled=True),
        lax.all_to_all(outgoing_ids, ("files", "clus"), split_axis=0, concat_axis=2, tiled=True),
    )
    blocks = blocks[0]
    block_ids = block_ids[0]
    start_best = jnp.full(block_ids.shape, -1.0, jnp.float32)
    similar, row_first, row_second = tile_maxima(
        blocks,
        block_ids,
        lax.all_gather(blocks, "clus", axis=1, tiled=True),
        lax.all_gather(block_ids, "clus", axis=1, tiled=True),
    )
    first_best = jnp.maximum(start_best, row_first)
    second_best = jnp.maximum(start_best, row_second)
    returned_first, returned_second = (
        lax.all_to_all(
            first_best[None], ("files", "clus"), split_axis=2, concat_axis=0, tiled=True
        ),
        lax.all_to_all(
            second_best[None], ("files", "clus"), split_axis=2, concat_axis=0, tiled=True
        ),
    )
    earlier_best = returned_first.reshape(-1)[flat]
    later_best = returned_second.reshape(-1)[flat]
    return (earlier_best, later_best)


def solution(mesh):
    placed = (P(("files", "clus"), None), P(("files", "clus"), None))
    return jax.shard_map(
        body,
        mesh=mesh,
        in_specs=placed,
        out_specs=(P(("files", "clus")), P(("files", "clus"))),
        check_vma=False,
    )
```

profile of v0, /device:TPU:1, one launch (start us, length us, event | category | flops | bytes accessed | tf_op | source)
XLA Modules:
  0.0 246.9 jit_solution(12458865414547434104)
XLA Ops:
  7.2 0.0 copy-start.1
  7.2 0.0 copy-start.2
  7.2 0.0 all-gather.2.cloned.1.call-start
  7.2 1.6 fusion
  8.8 0.7 fusion.9
  9.5 18.0 %reduce-window.6 = s32[64,8,128]{2,1,0:T(8,128)S(1)} reduce-window(s32[64,8,128]{2,1,0:T(8,128)S(1)} %fusion.9, s32[]{:T(128)} %constant.65.clone.1), window={size=1x1x128 pad=0_0x0_0x127_0}, to_apply=%region_0.0 | reduce-window | flops 8323072 | bytes 524292 | tf_op jit(solution)/shard_map/reduce-window
  27.5 0.1 slice.12
  27.7 0.1 copy.19
  27.9 0.1 copy.20
  28.0 0.1 broadcast_add_fusion
  28.1 0.0 copy-done.2
  28.1 0.1 fusion.8
  28.2 0.1 compare_select_fusion
  28.3 0.0 copy-done.1
  28.3 6.2 %scatter_custom_fusion.1 = bf16[2048,512]{1,0:T(8,128)(2,1)S(1)} fusion(s32[1024]{0:T(1024)S(1)} %bitcast.57, bf16[1024,512]{1,0:T(8,128)(2,1)S(1)} %copy-done.1, f32[1024]{0:T(1024)S(1)} %add_rsqrt_fusion, bf16[]{:T(256)} %constant.76.clone.1), kind=kCustom, calls=%fused_computation.10 | custom fusion | flops 1572864 | bytes 3149826 | tf_op jit(solution)/shard_map/scatter | solution.py:41
  34.5 2.1 reshape.138
  36.5 42.0 %all_to_all.60 = bf16[128,4,4,512]{3,2,1,0:T(4,128)(2,1)S(1)} all-to-all(bf16[128,4,4,512]{3,2,1,0:T(4,128)(2,1)} %reshape.138), channel_id=1, replica_groups=mesh['files'=16,'clus'=8] {'files','clus'}, dimensions={0} | all-to-all | bytes 4194304 | tf_op jit(solution)/shard_map/all_to_all | solution.py:46
  78.6 0.7 copy.22
  79.3 2.1 squeeze.8
  81.4 0.0 copy-start
  81.4 0.0 all-gather.2.cloned.1.call-update
  81.4 4.3 %scatter_custom_fusion = s32[2048]{0:T(1024)S(1)} fusion(s32[1024]{0:T(1024)S(1)} %bitcast.58, s32[1024]{0:T(1024)S(1)} %iota_add_fusion, s32[]{:T(128)} %constant.63.clone.1), kind=kCustom, calls=%fused_computation.39 | custom fusion | bytes 8196 | tf_op jit(solution)/shard_map/scatter | solution.py:42
  85.8 0.3 reshape.137
  86.1 17.2 %all_to_all.61 = s32[128,4,4]{2,1,0:T(4,128)S(1)} all-to-all(s32[128,4,4]{2,1,0:T(4,128)S(1)} %reshape.137), channel_id=1, replica_groups=mesh['files'=16,'clus'=8] {'files','clus'}, dimensions={0} | all-to-all | bytes 16384 | tf_op jit(solution)/shard_map/all_to_all | solution.py:47
  103.4 0.2 squeeze.7
  103.5 14.1 %all_gather.6 = s32[4,4096]{1,0:T(4,128)S(1)} all-gather(s32[4,512]{1,0:T(4,128)S(1)} %squeeze.7), channel_id=1, replica_groups=mesh['files'=16,'clus'=8] {'clus'}, dimensions={1}, use_global_device_ids=true | all-gather | bytes 73728 | tf_op jit(solution)/shard_map/all_gather | solution.py:56
  117.7 47.8 %all-gather.2.cloned.1.call-done = bf16[4,4096,512]{2,1,0:T(8,128)(2,1)} async-done(((bf16[4,512,512]{2,1,0:T(8,128)(2,1)}), bf16[4,4096,512]{2,1,0:T(8,128)(2,1)}) %all-gather.2.cloned.1.call-update) | async-done | bytes 16777232 | tf_op jit(solution)/shard_map/all_gather | solution.py:55
  165.5 0.0 copy-done
  165.5 16.4 %select_reduce_fusion = (f32[4,512]{1,0:T(4,128)S(1)}, f32[4,512]{1,0:T(4,128)S(1)}) fusion(s32[4,512]{1,0:T(4,128)S(1)} %squeeze.7, s32[4,4096]{1,0:T(4,128)S(1)} %all_gather.6, pred[4,4096]{1,0:T(4,128)(4,1)S(1)} %broadcast_compare_fusion, bf16[4,512,512]{2,1,0:T(8,128)(2,1)S(1)} %copy-done, bf16[4,4096,512]{2,1,0:T(8,128)(2,1)} %all-gather.2.cloned.1.call-done), kind=kOutput, calls=%fused_computation.4 | convolution fusion | flops 8648650752 | bytes 18980864 | tf_op jit(solution)/shard_map/qmd,qnd->qmn/dot_general | solution.py:11
  181.9 0.9 copy.23
  182.7 8.1 %all-to-all-start.2 = ((f32[1,4,512]{1,0,2:T(1,128)}), f32[1,4,512]{1,0,2:T(1,128)S(1)}, u32[]{:S(2)}, u32[]{:S(2)}) async-start(f32[1,4,512]{1,0,2:T(1,128)} %copy.23), calls=%async_computation.2 | async-start | bytes 524288 | tf_op jit(solution)/shard_map/all_to_all | solution.py:61
  190.8 0.9 copy.26
  191.7 10.2 %all-to-all-done.2 = f32[1,4,512]{1,0,2:T(1,128)S(1)} async-done(((f32[1,4,512]{1,0,2:T(1,128)}), f32[1,4,512]{1,0,2:T(1,128)S(1)}, u32[]{:S(2)}, u32[]{:S(2)}) %all-to-all-start.2) | async-done | bytes 8224 | tf_op jit(solution)/shard_map/all_to_all | solution.py:61
  201.9 4.4 %all-to-all-start.3 = ((f32[1,4,512]{1,0,2:T(1,128)}), f32[1,4,512]{1,0,2:T(1,128)S(1)}, u32[]{:S(2)}, u32[]{:S(2)}) async-start(f32[1,4,512]{1,0,2:T(1,128)} %copy.26), calls=%async_computation.3 | async-start | bytes 524288 | tf_op jit(solution)/shard_map/all_to_all | solution.py:64
  206.4 1.0 copy.29
  207.4 0.2 copy.25
  207.6 0.3 reshape.139
  207.8 9.6 %all-to-all-done.3 = f32[1,4,512]{1,0,2:T(1,128)S(1)} async-done(((f32[1,4,512]{1,0,2:T(1,128)}), f32[1,4,512]{1,0,2:T(1,128)S(1)}, u32[]{:S(2)}, u32[]{:S(2)}) %all-to-all-start.3) | async-done | bytes 8224 | tf_op jit(solution)/shard_map/all_to_all | solution.py:64
  217.5 1.0 copy.30
  218.5 0.2 copy.28
  218.7 0.3 reshape.140
  218.9 10.5 %gather_fusion = f32[1024]{0:T(1024)} fusion(f32[2048]{0:T(1024)S(1)} %reshape.139, s32[1024]{0:T(1024)S(1)} %broadcast_clamp_fusion), kind=kCustom, calls=%fused_computation | custom fusion | bytes 12288 | tf_op jit(solution)/shard_map/gather | solution.py:68
  229.5 10.5 %gather_fusion.1 = f32[1024]{0:T(1024)} fusion(f32[2048]{0:T(1024)S(1)} %reshape.140, s32[1024]{0:T(1024)S(1)} %broadcast_clamp_fusion), kind=kCustom, calls=%fused_computation.1 | custom fusion | bytes 12288 | tf_op jit(solution)/shard_map/gather | solution.py:69
  (9 shorter events, 0.1 us)
Async XLA Ops:
  7.2 21.1 %copy-start.1 = (bf16[1024,512]{1,0:T(8,128)(2,1)S(1)}, bf16[1024,512]{1,0:T(8,128)(2,1)}, u32[]{:S(2)}) copy-start(bf16[1024,512]{1,0:T(8,128)(2,1)} %param.2) | copy-start | bytes 3145732
  7.2 20.9 %copy-start.2 = (s32[1024,1]{0,1:T(1,128)S(1)}, s32[1024,1]{0,1:T(1,128)}, u32[]{:S(2)}) copy-start(s32[1024,1]{0,1:T(1,128)} %param.3) | copy-start | bytes 12292
  7.2 158.3 %all-gather.2.cloned.1.call-start = ((), (), s32[]{:S(2)}) async-start(), calls=%async_computation.4 | async-start | bytes 18874368 | tf_op jit(solution)/shard_map/all_gather | solution.py:55
  81.4 84.1 %copy-start = (bf16[4,512,512]{2,1,0:T(8,128)(2,1)S(1)}, bf16[4,512,512]{2,1,0:T(8,128)(2,1)}, u32[]{:S(2)}) copy-start(bf16[4,512,512]{2,1,0:T(8,128)(2,1)} %squeeze.8) | copy-start | bytes 6291460
  182.7 19.2 %all-to-all-start.2 = ((f32[1,4,512]{1,0,2:T(1,128)}), f32[1,4,512]{1,0,2:T(1,128)S(1)}, u32[]{:S(2)}, u32[]{:S(2)}) async-start(f32[1,4,512]{1,0,2:T(1,128)} %copy.23), calls=%async_computation.2 | async-start | bytes 524288 | tf_op jit(solution)/shard_map/all_to_all | solution.py:61
  201.9 15.5 %all-to-all-start.3 = ((f32[1,4,512]{1,0,2:T(1,128)}), f32[1,4,512]{1,0,2:T(1,128)S(1)}, u32[]{:S(2)}, u32[]{:S(2)}) async-start(f32[1,4,512]{1,0,2:T(1,128)} %copy.26), calls=%async_computation.3 | async-start | bytes 524288 | tf_op jit(solution)/shard_map/all_to_all | solution.py:64
Sparse Core Ops, SparseCore 0:
  81.5 83.8 all-gather.1
where the time goes:
time: 247 us
  blocking collectives  73.3 us (30%)
  waiting for transfers between devices  67.7 us (27%)
  local copies, waits for them, and re-layouts  35.8 us (14%)
  other arithmetic  26.8 us (11%)
  matrix products  16.4 us (7%)
  between operations  14.2 us (6%)
  starting transfers between devices  12.6 us (5%)
    all_gather x1, waiting for transfers between devices, body(): lax.all_gather(blocks, 'clus', axis=1, tiled=True)  47.8 us
    all_to_all x1, blocking collectives, body(): lax.all_to_all(outgoing, ('files', 'clus'), split_axis=0, concat_axis=2,...  42 us
    another operation x3, other arithmetic  18.2 us
    all_to_all x1, blocking collectives, body(): lax.all_to_all(outgoing_ids, ('files', 'clus'), split_axis=0, concat_axis...  17.2 us
    dot_general x1, matrix products, tile_maxima(): jnp.einsum('qmd,qnd->qmn', own, other, preferred_element_type=jnp.float32)  16.4 us
    all_gather x1, blocking collectives, body(): lax.all_gather(block_ids, 'clus', axis=1, tiled=True)  14.1 us
    gather x1, local copies, waits for them, and re-layouts, body(): earlier_best = returned_first.reshape(-1)[flat]  10.5 us
    gather x1, local copies, waits for them, and re-layouts, body(): later_best = returned_second.reshape(-1)[flat]  10.5 us
  transfers between devices with their start and end apart: 3, of which 3 were waited for; matrix products, arithmetic and copies ran while one was open for 3% of the time, Pallas kernels for 0%

commit v1 on v0

v1 whole, which is shorter than its diff:
```python
import jax
import jax.numpy as jnp
from jax import lax
from jax.experimental import pallas as pl
from jax.experimental.pallas import tpu as pltpu
from jax.sharding import PartitionSpec as P

MESH = pl.DeviceIdType.MESH
SIDE = 4
CHIPS = SIDE**3
CAP = 32
WIDTH = 512
ROWS = 1024
LANES = 128
PHASES = 8
PER = CHIPS // PHASES
BLOCK = PER * CAP
EMPTY = 2.0
NT = (((1,), (1,)), ((), ()))


def kernel(
    emb_ref, lab_ref, first_ref, second_ref,
    raw, unit, outgoing, own, other, acc, bias, res, ret, turned, onehot, rank_s, key_s, count_s,
    raw_sem, self_sem, send_sem, recv_sem, fwd_send, fwd_recv, ret_send, ret_recv,
):
    files, clus = lax.axis_index("files"), lax.axis_index("clus")
    z, y, x, core = files // SIDE, files % SIDE, clus // 2, clus % 2
    chip = (z * SIDE + y) * SIDE + x

    def device(cz, cy, cx, ck):
        return (cz * SIDE + cy, cx * 2 + ck)

    def wrap(v):
        return lax.rem(v + SIDE, SIDE)

    partner = device(z, y, x, 1 - core)
    load = pltpu.make_async_copy(emb_ref, raw, raw_sem)
    load.start()

    barrier = pltpu.get_barrier_semaphore()
    pl.semaphore_signal(barrier, inc=1, device_id=partner, device_id_type=MESH)

    @pl.loop(1, CHIPS)
    def _(i):
        target = device(wrap(z + i // 16), wrap(y + i // 4 % 4), wrap(x + i % 4), core)
        pl.semaphore_signal(barrier, inc=1, device_id=target, device_id_type=MESH)

    labels = lab_ref[...]
    cluster = lax.broadcasted_iota(jnp.int32, (CHIPS, LANES), 0)
    blocks = ROWS // LANES
    hot = [
        jnp.where(labels[:, b * LANES : (b + 1) * LANES] == cluster, 1.0, 0.0) for b in range(blocks)
    ]
    earlier = jnp.where(
        lax.broadcasted_iota(jnp.int32, (LANES, LANES), 0)
        < lax.broadcasted_iota(jnp.int32, (LANES, LANES), 1),
        1.0,
        0.0,
    ).astype(jnp.bfloat16)
    within = jnp.dot(
        jnp.concatenate(hot, axis=0).astype(jnp.bfloat16), earlier, preferred_element_type=jnp.float32
    )
    carry = jnp.zeros((CHIPS, 1), jnp.float32)
    for b in range(blocks):
        lanes = slice(b * LANES, (b + 1) * LANES)
        rank = jnp.sum(
            hot[b] * (within[b * CHIPS : (b + 1) * CHIPS] + carry), axis=0, keepdims=True
        ).astype(jnp.int32)
        rank_s[:, lanes] = rank
        key_s[:, lanes] = labels[:, lanes] * CAP + rank
        onehot[:, lanes] = hot[b].astype(jnp.bfloat16)
        carry = carry + jnp.sum(hot[b], axis=1, keepdims=True)
    count_s[...] = jnp.broadcast_to(carry, (CHIPS, LANES)).astype(jnp.int32)

    load.wait()

    @pl.loop(0, 4)
    def _(i):
        rows = pl.ds(i * (ROWS // 4), ROWS // 4)
        e = raw[rows, :].astype(jnp.float32)
        squares = jnp.sum(e * e, axis=1, keepdims=True) + 1e-06
        unit[rows, :] = (e * lax.rsqrt(squares)).astype(jnp.bfloat16)

    def send(i, stage_x):
        target = device(wrap(z + i // 16), wrap(y + i // 4 % 4), wrap(x + i % 4), core)
        return pltpu.make_async_remote_copy(
            src_ref=outgoing.at[i],
            dst_ref=own.at[stage_x],
            send_sem=send_sem,
            recv_sem=recv_sem.at[i // PER],
            device_id=target,
            device_id_type=MESH,
        )

    keep = pltpu.make_async_copy(outgoing.at[0], own.at[x], self_sem)

    def pack(phase):
        key = key_s[...]
        slot = lax.broadcasted_iota(jnp.int32, (CAP, ROWS), 0)
        picks, holes = [], []
        for j in range(PER):
            i = phase * PER + j
            c = (wrap(z + i // 16) * SIDE + wrap(y + i // 4 % 4)) * SIDE + wrap(x + i % 4)
            picks.append(jnp.where(key - c * CAP == slot, 1.0, 0.0).astype(jnp.bfloat16))
            holes.append(
                (lax.broadcasted_iota(jnp.int32, (CAP, LANES), 0) >= count_s[pl.ds(c, 1), :])
                & (lax.broadcasted_iota(jnp.int32, (CAP, LANES), 1) == 0)
            )
        rows = jnp.dot(jnp.concatenate(picks, axis=0), unit[...], preferred_element_type=jnp.float32)
        for j in range(PER):
            i = phase * PER + j
            part = rows[j * CAP : (j + 1) * CAP]
            outgoing[i, :, :LANES] = jnp.where(holes[j], EMPTY, part[:, :LANES]).astype(jnp.bfloat16)
            outgoing[i, :, LANES:] = part[:, LANES:].astype(jnp.bfloat16)

    pack(0)
    pl.semaphore_wait(barrier, CHIPS)
    keep.start()
    for i in range(1, PER):
        send(i, i // 4 * 4 + x).start()

    @pl.loop(1, PHASES)
    def _(phase):
        pack(phase)
        for j in range(PER):
            i = phase * PER + j
            send(i, i // 4 * 4 + x).start()

    acc[...] = jnp.full(acc.shape, -1.0, jnp.float32)

    def place(phase, half):
        return wrap(z - phase // 2) * SIDE + wrap(y - (phase % 2 * 2 + half))

    def block(ref, phase):
        return ref[pl.ds(phase * PER, PER)].reshape(BLOCK, WIDTH)

    def set_bias(ref, phase, side):
        head = ref[pl.ds(phase * PER, PER), :, pl.ds(0, LANES)].reshape(BLOCK, LANES)
        mark = jnp.transpose(head.astype(jnp.float32))[0:1, :]
        bias[phase * 2 + side] = jnp.where(mark > 1.5, -4.0, 0.0)

    def cross(rows, row_phase, cols, col_phase, side):
        similar = lax.dot_general(rows, cols, NT, preferred_element_type=jnp.float32)
        similar = similar + bias[col_phase * 2 + side]
        for i in range(2):
            for j in range(2):
                after = jnp.where(place(col_phase, j) < place(row_phase, i), 0, 1)
                part = similar[i * LANES : (i + 1) * LANES, j * LANES : (j + 1) * LANES]
                at = pl.ds(pl.multiple_of(row_phase * BLOCK + i * LANES, LANES), LANES)
                acc[after, at, :] = jnp.maximum(acc[after, at, :], part)

    def order(phase, dim, ck):
        r = lax.broadcasted_iota(jnp.int32, (BLOCK, BLOCK), dim)
        group = jnp.where(r < LANES, place(phase, 0), place(phase, 1))
        return group * (2 * LANES) + r % LANES // CAP * (2 * CAP) + ck * CAP + r % CAP

    def diagonal(rows, cols, phase, side):
        similar = lax.dot_general(rows, cols, NT, preferred_element_type=jnp.float32)
        similar = similar + bias[phase * 2 + side]
        mine = order(phase, 0, core)
        theirs = order(phase, 1, jnp.where(side == 0, core, 1 - core))
        at = pl.ds(pl.multiple_of(phase * BLOCK, BLOCK), BLOCK)
        for after in range(2):
            mask = theirs < mine if after == 0 else theirs > mine
            part = jnp.where(mask, similar, -1.0)
            part = jnp.maximum(part[:, :LANES], part[:, LANES:])
            acc[after, at, :] = jnp.maximum(acc[after, at, :], part)

    def forward(phase):
        at = pl.ds(phase * PER, PER)
        return pltpu.make_async_remote_copy(
            src_ref=own.at[at],
            dst_ref=other.at[at],
            send_sem=fwd_send.at[phase],
            recv_sem=fwd_recv.at[phase],
            device_id=partner,
            device_id_type=MESH,
        )

    def arrived(first, number, phase):
        at = pl.ds(first, number)
        pltpu.make_async_remote_copy(
            src_ref=own.at[at],
            dst_ref=own.at[at],
            send_sem=send_sem,
            recv_sem=recv_sem.at[phase],
            device_id=partner,
            device_id_type=MESH,
        ).wait_recv()

    def work(phase):
        forward(phase).start()
        set_bias(own, phase, 0)
        mine = block(own, phase)

        @pl.loop(0, phase)
        def _(u):
            past = block(own, u)
            cross(past, u, mine, phase, 0)
            cross(mine, phase, past, u, 0)
            cross(mine, phase, block(other, u), u, 1)

        diagonal(mine, mine, phase, 0)
        forward(phase).wait_recv()
        set_bias(other, phase, 1)
        theirs = block(other, phase)

        @pl.loop(0, phase)
        def _(u):
            cross(block(own, u), u, theirs, phase, 1)

        diagonal(mine, theirs, phase, 1)

    keep.wait()
    arrived(0, PER - 1, 0)
    work(0)

    @pl.loop(1, PHASES)
    def _(phase):
        arrived(phase * PER, PER, phase)
        work(phase)

    def give(i):
        target = device(wrap(z - i // 16), wrap(y - i // 4 % 4), wrap(x + i % 4), core)
        return pltpu.make_async_remote_copy(
            src_ref=res.at[i // 4],
            dst_ref=ret.at[chip],
            send_sem=ret_send,
            recv_sem=ret_recv,
            device_id=target,
            device_id_type=MESH,
        )

    def finish(stage):
        at = pl.ds(pl.multiple_of(stage * LANES, LANES), LANES)
        for after in range(2):
            best = jnp.max(jnp.transpose(acc[after, at, :]), axis=0, keepdims=True)
            res[stage, after : after + 1, :] = best

    finish(0)
    ret[chip] = res[0]
    for i in range(1, 4):
        give(i).start()

    @pl.loop(1, CHIPS // 4)
    def _(stage):
        finish(stage)
        for j in range(4):
            give(stage * 4 + j).start()

    back = pltpu.make_async_remote_copy(
        src_ref=ret.at[pl.ds(0, CHIPS - 1)],
        dst_ref=ret.at[pl.ds(0, CHIPS - 1)],
        send_sem=ret_send,
        recv_sem=ret_recv,
        device_id=partner,
        device_id_type=MESH,
    )
    back.wait_recv()

    for after in range(2):
        turned[after] = jnp.transpose(ret[:, after, :])
    pieces = []
    for after in range(2):
        rest = turned[after, pl.ds(pl.multiple_of(x * CAP, CAP), CAP), :]
        for _ in range(3):
            piece = rest.astype(jnp.bfloat16)
            pieces.append(piece)
            rest = rest - piece.astype(jnp.float32)
    table = jnp.dot(
        jnp.concatenate(pieces, axis=0), onehot[...], preferred_element_type=jnp.float32
    )
    chosen = lax.broadcasted_iota(jnp.int32, (CAP, ROWS), 0) == rank_s[...]
    for after, out in enumerate((first_ref, second_ref)):
        t = table[after * 3 * CAP : (after + 1) * 3 * CAP]
        value = t[:CAP] + t[CAP : 2 * CAP] + t[2 * CAP :]
        value = jnp.sum(jnp.where(chosen, value, 0.0), axis=0, keepdims=True)
        for b in range(blocks):
            out[b : b + 1, :] = value[:, b * LANES : (b + 1) * LANES]

    back.wait_send()
    pltpu.make_async_remote_copy(
        src_ref=outgoing.at[pl.ds(1, CHIPS - 1)],
        dst_ref=outgoing.at[pl.ds(1, CHIPS - 1)],
        send_sem=send_sem,
        recv_sem=recv_sem.at[0],
        device_id=partner,
        device_id_type=MESH,
    ).wait_send()

    @pl.loop(0, PHASES)
    def _(phase):
        forward(phase).wait_send()


def body(embeddings, cluster_ids):
    vmem = pl.BlockSpec(memory_space=pltpu.VMEM)
    shape = jax.ShapeDtypeStruct((ROWS // LANES, LANES), jnp.float32)
    first, second = pl.pallas_call(
        kernel,
        out_shape=(shape, shape),
        in_specs=[pl.BlockSpec(memory_space=pl.ANY), vmem],
        out_specs=(vmem, vmem),
        scratch_shapes=[
            pltpu.VMEM((ROWS, WIDTH), jnp.bfloat16),
            pltpu.VMEM((ROWS, WIDTH), jnp.bfloat16),
            pltpu.VMEM((CHIPS, CAP, WIDTH), jnp.bfloat16),
            pltpu.VMEM((CHIPS, CAP, WIDTH), jnp.bfloat16),
            pltpu.VMEM((CHIPS, CAP, WIDTH), jnp.bfloat16),
            pltpu.VMEM((2, CHIPS * CAP, LANES), jnp.float32),
            pltpu.VMEM((PHASES * 2, 1, BLOCK), jnp.float32),
            pltpu.VMEM((CHIPS // 4, 2, LANES), jnp.float32),
            pltpu.VMEM((CHIPS, 2, LANES), jnp.float32),
            pltpu.VMEM((2, LANES, CHIPS), jnp.float32),
            pltpu.VMEM((CHIPS, ROWS), jnp.bfloat16),
            pltpu.VMEM((1, ROWS), jnp.int32),
            pltpu.VMEM((1, ROWS), jnp.int32),
            pltpu.VMEM((CHIPS, LANES), jnp.int32),
            pltpu.SemaphoreType.DMA,
            pltpu.SemaphoreType.DMA,
            pltpu.SemaphoreType.DMA,
            pltpu.SemaphoreType.DMA((PHASES,)),
            pltpu.SemaphoreType.DMA((PHASES,)),
            pltpu.SemaphoreType.DMA((PHASES,)),
            pltpu.SemaphoreType.DMA,
            pltpu.SemaphoreType.DMA,
        ],
        compiler_params=pltpu.CompilerParams(
            collective_id=0, has_side_effects=True, vmem_limit_bytes=40 << 20
        ),
        cost_estimate=pl.CostEstimate(
            flops=2 * (2048 * 4096 + 2048 * 1024) * WIDTH, bytes_accessed=2 << 20, transcendentals=ROWS
        ),
    )(embeddings, cluster_ids.reshape(1, ROWS))
    return (first.reshape(ROWS), second.reshape(ROWS))


def solution(mesh):
    placed = (P(("files", "clus"), None), P(("files", "clus"), None))
    return jax.shard_map(
        body,
        mesh=mesh,
        in_specs=placed,
        out_specs=(P(("files", "clus")), P(("files", "clus"))),
        check_vma=False,
    )
```

time: 247 us -> 74.3 us (0.30)
  blocking collectives: 73.3 us -> 0 us
  Pallas kernels: 0 us -> 70.3 us
  waiting for transfers between devices: 67.7 us -> 0 us
  local copies, waits for them, and re-layouts: 35.8 us -> 3.09 us
  other arithmetic: 26.8 us -> 0 us
  matrix products: 16.4 us -> 0 us
  between operations: 14.2 us -> 0.65 us
  starting transfers between devices: 12.6 us -> 0 us
    pallas_call x0 -> x1, Pallas kernels: none -> 70.3 us  [body(): pl.pallas_call(kernel, out_shape=(shape, shape), in_specs=[pl.BlockSpec(m...]
    all_to_all x2 -> x0, blocking collectives: 59.3 us -> none  [the longest x1 42 us: body(): lax.all_to_all(outgoing, ('files', 'clus'), split_axis=0, concat_axis=2,...]
    all_gather x1 -> x0, waiting for transfers between devices: 47.8 us -> none  [body(): lax.all_gather(blocks, 'clus', axis=1, tiled=True)]
    gather x2 -> x0, local copies, waits for them, and re-layouts: 21.1 us -> none  [the longest x1 10.5 us: body(): earlier_best = returned_first.reshape(-1)[flat]]
    all_to_all x2 -> x0, waiting for transfers between devices: 19.8 us -> none  [the longest x1 10.2 us: body(): lax.all_to_all(first_best[None], ('files', 'clus'), split_axis=2, concat_...]
    another operation x5 -> x0, other arithmetic: 18.2 us -> none
    dot_general x1 -> x0, matrix products: 16.4 us -> none  [tile_maxima(): jnp.einsum('qmd,qnd->qmn', own, other, preferred_element_type=jnp.float32)]
    all_gather x1 -> x0, blocking collectives: 14.1 us -> none  [body(): lax.all_gather(block_ids, 'clus', axis=1, tiled=True)]
  transfers between devices with their start and end apart: 3 -> 0, of which waited for: 3 -> 0; matrix products, arithmetic and copies ran while one was open for 3% -> 0% of each run, Pallas kernels for 0% -> 0%
where the time goes in v1:
time: 74.3 us; the launch traced here: 74.1 us
  Pallas kernels  70.3 us (95%)
  local copies, waits for them, and re-layouts  3.09 us (4%)
    pallas_call x1, Pallas kernels, body(): pl.pallas_call(kernel, out_shape=(shape, shape), in_specs=[pl.BlockSpec(m...  70.3 us
    unnamed x6, local copies, waits for them, and re-layouts  3.09 us

profile of v1, /device:TPU:1, one launch (start us, length us, event | category | flops | bytes accessed | tf_op | source)
XLA Modules:
  0.0 74.1 jit_solution(2101048298637575617)
XLA Ops:
  0.6 0.0 copy-start
  0.6 1.2 %copy-done = bf16[1024,512]{1,0:T(8,128)(2,1)S(1)} copy-done((bf16[1024,512]{1,0:T(8,128)(2,1)S(1)}, bf16[1024,512]{1,0:T(8,128)(2,1)}, u32[]{:S(2)}) %copy-start) | copy-done | bytes 1048600
  1.9 0.0 copy-start.1
  1.9 0.7 copy-done.1
  2.5 70.3 %shard_map.41 = (f32[8,128]{1,0:T(8,128)S(1)}, f32[8,128]{1,0:T(8,128)S(1)}) custom-call(bf16[1024,512]{1,0:T(8,128)(2,1)S(1)} %copy-done, s32[1,1024]{1,0:T(1,128)S(1)} %bitcast.5), custom_call_target="tpu_custom_call" | custom-call | flops 10737418240 | bytes 2097152 | tf_op jit(solution)/shard_map/pallas_call | solution.py:300
  72.9 0.6 copy.6
  73.5 0.6 copy.7
Async XLA Ops:
  0.6 1.2 %copy-start = (bf16[1024,512]{1,0:T(8,128)(2,1)S(1)}, bf16[1024,512]{1,0:T(8,128)(2,1)}, u32[]{:S(2)}) copy-start(bf16[1024,512]{1,0:T(8,128)(2,1)} %emb_ref.1) | copy-start | bytes 3145732
  1.9 0.7 copy-start.1

commit v2 on v0

v2 whole, which is shorter than its diff:
```python
import jax
import jax.numpy as jnp
from jax import lax
from jax.experimental import pallas as pl
from jax.experimental.pallas import tpu as pltpu
from jax.sharding import PartitionSpec as P

MESH = pl.DeviceIdType.MESH
CHIPS = 64
CAP = 32
WIDTH = 512
ROWS = 1024
LANES = 128
PHASES = 8
PER = CHIPS // PHASES
BLOCK = PER * CAP


def offsets(t, j):
    a = -j % 4
    return (a + t % 4) % 4, (a + 2 * (j // 4) + t // 4) % 4, a


EMPTY = 2.0
NT = (((1,), (1,)), ((), ()))


def kernel(
    emb_ref, lab_ref, out_ref,
    raw, lab, unit, outgoing, own, other, acc, cacc, bias_l, bias_s, masks, orders, res, ret, turned,
    onehot, rank_s, key_s, count_s,
    raw_sem, lab_sem, self_sem, send_sem, recv_sem, fwd_send, fwd_recv, ret_send, ret_recv,
    ring_send, ring_recv,
):
    load = pltpu.make_async_copy(emb_ref, raw, raw_sem)
    load.start()
    load_lab = pltpu.make_async_copy(lab_ref, lab, lab_sem)
    load_lab.start()

    files, clus = lax.axis_index("files"), lax.axis_index("clus")
    z, y = lax.div(files, 4), lax.rem(files, 4)
    x, core = lax.div(clus, 2), lax.rem(clus, 2)
    here = x * 16 + files

    def wrap(v):
        return jnp.where(v >= 4, v - 4, v)

    zs, ys, xs = [[wrap(v + d) for d in range(4)] for v in (z, y, x)]
    partner = (files, clus + 1 - 2 * core)

    def target(t, j):
        dz, dy, dx = offsets(t, j)
        return (zs[dz] * 4 + ys[dy], xs[dx] * 2 + core)

    barrier = pltpu.get_barrier_semaphore()
    for t in range(PHASES):
        for j in range(PER):
            to = target(t, j) if t or j else partner
            pl.semaphore_signal(barrier, inc=1, device_id=to, device_id_type=MESH)

    cluster = lax.broadcasted_iota(jnp.int32, (CHIPS, LANES), 0)
    blocks = ROWS // LANES
    earlier = jnp.where(
        lax.broadcasted_iota(jnp.int32, (LANES, LANES), 0)
        < lax.broadcasted_iota(jnp.int32, (LANES, LANES), 1),
        1.0,
        0.0,
    ).astype(jnp.bfloat16)
    load_lab.wait()
    labels = lab[...]
    labels = labels % 4 * 16 + labels // 4
    hot = [
        jnp.where(labels[:, b * LANES : (b + 1) * LANES] == cluster, 1.0, 0.0) for b in range(blocks)
    ]
    within = jnp.dot(
        jnp.concatenate(hot, axis=0).astype(jnp.bfloat16), earlier, preferred_element_type=jnp.float32
    )
    carry = jnp.zeros((CHIPS, 1), jnp.float32)
    for b in range(blocks):
        lanes = slice(b * LANES, (b + 1) * LANES)
        rank = jnp.sum(
            hot[b] * (within[b * CHIPS : (b + 1) * CHIPS] + carry), axis=0, keepdims=True
        ).astype(jnp.int32)
        rank_s[:, lanes] = rank
        key_s[:, lanes] = labels[:, lanes] * CAP + rank
        onehot[:, lanes] = hot[b].astype(jnp.bfloat16)
        carry = carry + jnp.sum(hot[b], axis=1, keepdims=True)
    count_s[...] = jnp.broadcast_to(carry, (CHIPS, LANES)).astype(jnp.int32)

    load.wait()
    for i in range(4):
        rows = slice(i * (ROWS // 4), (i + 1) * (ROWS // 4))
        e = raw[rows, :].astype(jnp.float32)
        squares = jnp.sum(e * e, axis=1, keepdims=True) + 1e-06
        unit[rows, :] = (e * lax.rsqrt(squares)).astype(jnp.bfloat16)

    def send(t, j):
        return pltpu.make_async_remote_copy(
            src_ref=outgoing.at[t, j],
            dst_ref=own.at[t, j],
            send_sem=send_sem,
            recv_sem=recv_sem.at[t],
            device_id=target(t, j),
            device_id_type=MESH,
        )

    keep = pltpu.make_async_copy(outgoing.at[0, 0], own.at[0, 0], self_sem)

    def pack(t):
        key = key_s[...]
        slot = lax.broadcasted_iota(jnp.int32, (CAP, ROWS), 0)
        row = lax.broadcasted_iota(jnp.int32, (CAP, LANES), 0)
        lane = lax.broadcasted_iota(jnp.int32, (CAP, LANES), 1)
        picks, holes = [], []
        for j in range(PER):
            dz, dy, dx = offsets(t, j)
            c = xs[dx] * 16 + zs[dz] * 4 + ys[dy]
            picks.append(jnp.where(key - c * CAP == slot, 1.0, 0.0).astype(jnp.bfloat16))
            holes.append((row >= count_s[pl.ds(c, 1), :]) & (lane == 0))
        rows = jnp.dot(jnp.concatenate(picks, axis=0), unit[...], preferred_element_type=jnp.float32)
        for j in range(PER):
            part = rows[j * CAP : (j + 1) * CAP]
            outgoing[t, j, :, :LANES] = jnp.where(holes[j], EMPTY, part[:, :LANES]).astype(jnp.bfloat16)
            outgoing[t, j, :, LANES:] = part[:, LANES:].astype(jnp.bfloat16)

    for t in range(PHASES):
        pack(t)
        if t == 0:
            pl.semaphore_wait(barrier, CHIPS)
            keep.start()
        for j in range(PER):
            if t or j:
                send(t, j).start()

    def chip_order(t, j):
        a = -j % 4
        sz = (z - a - t % 4) % 4
        sy = (y - a - 2 * (j // 4) - t // 4) % 4
        return sz * 16 + sy * 4 + (x + j) % 4

    i = lax.broadcasted_iota(jnp.int32, (CHIPS, LANES), 0)
    orders[...] = chip_order(i // PER, i % PER)
    lane_j = lax.broadcasted_iota(jnp.int32, (1, BLOCK), 1) // CAP
    row_i = lax.broadcasted_iota(jnp.int32, (BLOCK, LANES), 0)

    def rows_of(ref, first, last):
        return ref[first:last].reshape((last - first) * BLOCK, WIDTH)

    def product(a, b):
        return lax.dot_general(a, b, NT, preferred_element_type=jnp.float32)

    def set_bias(ref, t, side):
        head = ref[t, :, :, :LANES].reshape(BLOCK, LANES).astype(jnp.float32)
        mark = jnp.broadcast_to(jnp.where(head[:, 0:1] > 1.5, -4.0, 0.0), (BLOCK, LANES))
        bias_s[side, t] = mark
        bias_l[t * 2 + side] = jnp.transpose(mark)[0:1, :]

        if t:
            columns = chip_order(t, lane_j)
            rows = orders[: t * PER, 0:1]
            masks[side, 0, : t * PER, :] = jnp.where(columns < rows, bias_l[t * 2 + side], -4.0)
            masks[side, 1, : t * PER, :] = jnp.where(columns > rows, bias_l[t * 2 + side], -4.0)

    def halves(part):
        return jnp.maximum(part[:, :LANES], part[:, LANES:])

    def maxima(similar, t, side, row_side, rowwise, best):
        for i in range(t * PER):
            u, at = i // PER, slice(i % PER * CAP, (i % PER + 1) * CAP)
            part = similar[i * CAP : (i + 1) * CAP]
            if best is not None:
                mark = bias_s[row_side, u, at, :]
                part = jnp.concatenate([part[:, :LANES] + mark, part[:, LANES:] + mark], axis=1)
            for after in range(2):
                kept = part + masks[side, after, i : i + 1, :]
                if rowwise:
                    acc[after, u, at, :] = jnp.maximum(acc[after, u, at, :], halves(kept))
                if best is not None:
                    high = jnp.max(kept.reshape(CAP // 8, 8, BLOCK), axis=0)
                    best[1 - after] = jnp.maximum(best[1 - after], high)

    def diagonal(t, side):
        similar = product(rows_of(own, t, t + 1), rows_of(other if side else own, t, t + 1))
        similar = similar + bias_l[t * 2 + side]
        lane = lax.broadcasted_iota(jnp.int32, (1, BLOCK), 1)
        mine = (chip_order(t, row_i // CAP) * (2 * CAP) + row_i % CAP)[:, 0:1]
        theirs = chip_order(t, lane_j) * (2 * CAP) + lane % CAP
        if side:
            theirs = theirs + (1 - 2 * core) * CAP
        for after in range(2):
            mask = theirs > mine if after else theirs < mine
            part = halves(jnp.where(mask, similar, -1.0))
            if side:
                acc[after, t] = jnp.maximum(acc[after, t], part)
            else:
                acc[after, t] = jnp.maximum(part, -1.0)

    def forward(t):
        return pltpu.make_async_remote_copy(
            src_ref=own.at[t],
            dst_ref=other.at[t],
            send_sem=fwd_send.at[t],
            recv_sem=fwd_recv.at[t],
            device_id=partner,
            device_id_type=MESH,
        )

    def arrived(t):
        blocks_of = own.at[t] if t else own.at[t, pl.ds(0, PER - 1)]
        pltpu.make_async_remote_copy(
            src_ref=blocks_of,
            dst_ref=blocks_of,
            send_sem=send_sem,
            recv_sem=recv_sem.at[t],
            device_id=partner,
            device_id_type=MESH,
        ).wait_recv()

    for t in range(PHASES):
        if t == 0:
            keep.wait()
        arrived(t)
        forward(t).start()
        set_bias(own, t, 0)
        mine = rows_of(own, t, t + 1)
        best = [jnp.full((8, BLOCK), -1.0, jnp.float32)] * 2
        if t:
            maxima(product(rows_of(own, 0, t), mine), t, 0, 0, True, best)
            maxima(product(rows_of(other, 0, t), mine), t, 0, 1, False, best)
        for after in range(2):
            cacc[t, after] = best[after]
        diagonal(t, 0)
        forward(t).wait_recv()
        set_bias(other, t, 1)
        if t:
            maxima(product(rows_of(own, 0, t), rows_of(other, t, t + 1)), t, 1, 0, True, None)
        diagonal(t, 1)

    quarter = lax.broadcasted_iota(jnp.int32, (1, LANES), 1) // CAP
    lines = {}
    for t in range(PHASES):
        for after in range(2):
            best = jnp.max(jnp.transpose(acc[after, t]), axis=0, keepdims=True)
            best = jnp.maximum(best, jnp.max(cacc[t, after], axis=0, keepdims=True))
            for j in range(PER):
                dz, dy, dx = offsets(t, j)
                line = best[:, j // 4 * LANES : (j // 4 + 1) * LANES]
                key = (dz * 4 + dy, after)
                lines[key] = jnp.where(quarter == j % 4, line, lines[key]) if key in lines else line
    for i in range(16):
        for after in range(2):
            res[i, after : after + 1, :] = pltpu.roll(lines[i, after], x * CAP, 1)
        if i:
            give = pltpu.make_async_remote_copy(
                src_ref=res.at[i],
                dst_ref=ret.at[here],
                send_sem=ret_send,
                recv_sem=ret_recv,
                device_id=(zs[-(i // 4) % 4] * 4 + ys[-(i % 4) % 4], clus),
                device_id_type=MESH,
            )
            give.start()
    ret[here] = res[0]

    def tally(first, number, send_sem, recv_sem):
        return pltpu.make_async_remote_copy(
            src_ref=ret.at[pl.ds(first, number)],
            dst_ref=ret.at[pl.ds(first, number)],
            send_sem=send_sem,
            recv_sem=recv_sem,
            device_id=partner,
            device_id_type=MESH,
        )

    tally(0, 15, ret_send, ret_recv).wait_recv()
    column = ret.at[pl.ds(pl.multiple_of(x * 16, 16), 16)]
    for d in range(1, 4):
        pltpu.make_async_remote_copy(
            src_ref=column,
            dst_ref=column,
            send_sem=ring_send,
            recv_sem=ring_recv,
            device_id=(files, xs[d] * 2 + core),
            device_id_type=MESH,
        ).start()
    tally(0, 48, ring_send, ring_recv).wait_recv()

    for after in range(2):
        turned[after] = jnp.transpose(ret[:, after, :])
    pieces = []
    for after in range(2):
        rest = turned[after, pl.ds(pl.multiple_of(x * CAP, CAP), CAP), :]
        for _ in range(3):
            piece = rest.astype(jnp.bfloat16)
            pieces.append(piece)
            rest = rest - piece.astype(jnp.float32)
    table = jnp.dot(
        jnp.concatenate(pieces, axis=0), onehot[...], preferred_element_type=jnp.float32
    )
    chosen = lax.broadcasted_iota(jnp.int32, (CAP, ROWS), 0) == rank_s[...]
    for after in range(2):
        t = table[after * 3 * CAP : (after + 1) * 3 * CAP]
        value = t[:CAP] + t[CAP : 2 * CAP] + t[2 * CAP :]
        value = jnp.sum(jnp.where(chosen, value, 0.0), axis=0, keepdims=True)
        for b in range(blocks):
            out_ref[after, b : b + 1, :] = value[:, b * LANES : (b + 1) * LANES]

    tally(0, 15, ret_send, ret_recv).wait_send()
    tally(0, 48, ring_send, ring_recv).wait_send()
    sent = pltpu.make_async_remote_copy(
        src_ref=outgoing.at[0, pl.ds(0, PER - 1)],
        dst_ref=outgoing.at[0, pl.ds(0, PER - 1)],
        send_sem=send_sem,
        recv_sem=recv_sem.at[0],
        device_id=partner,
        device_id_type=MESH,
    )
    sent.wait_send()
    pltpu.make_async_remote_copy(
        src_ref=outgoing.at[pl.ds(1, PHASES - 1)],
        dst_ref=outgoing.at[pl.ds(1, PHASES - 1)],
        send_sem=send_sem,
        recv_sem=recv_sem.at[0],
        device_id=partner,
        device_id_type=MESH,
    ).wait_send()
    for t in range(PHASES):
        forward(t).wait_send()


def body(embeddings, cluster_ids):
    anywhere = pl.BlockSpec(memory_space=pl.ANY)
    out = pl.pallas_call(
        kernel,
        out_shape=jax.ShapeDtypeStruct((2, ROWS // LANES, LANES), jnp.float32),
        in_specs=[anywhere, anywhere],
        out_specs=pl.BlockSpec(memory_space=pltpu.VMEM),
        scratch_shapes=[
            pltpu.VMEM((ROWS, WIDTH), jnp.bfloat16),
            pltpu.VMEM((1, ROWS), jnp.int32),
            pltpu.VMEM((ROWS, WIDTH), jnp.bfloat16),
            pltpu.VMEM((PHASES, PER, CAP, WIDTH), jnp.bfloat16),
            pltpu.VMEM((PHASES, PER, CAP, WIDTH), jnp.bfloat16),
            pltpu.VMEM((PHASES, PER, CAP, WIDTH), jnp.bfloat16),
            pltpu.VMEM((2, PHASES, BLOCK, LANES), jnp.float32),
            pltpu.VMEM((PHASES, 2, 8, BLOCK), jnp.float32),
            pltpu.VMEM((PHASES * 2, 1, BLOCK), jnp.float32),
            pltpu.VMEM((2, PHASES, BLOCK, LANES), jnp.float32),
            pltpu.VMEM((2, 2, CHIPS, BLOCK), jnp.float32),
            pltpu.VMEM((CHIPS, LANES), jnp.int32),
            pltpu.VMEM((16, 2, LANES), jnp.float32),
            pltpu.VMEM((CHIPS, 2, LANES), jnp.float32),
            pltpu.VMEM((2, LANES, CHIPS), jnp.float32),
            pltpu.VMEM((CHIPS, ROWS), jnp.bfloat16),
            pltpu.VMEM((1, ROWS), jnp.int32),
            pltpu.VMEM((1, ROWS), jnp.int32),
            pltpu.VMEM((CHIPS, LANES), jnp.int32),
            pltpu.SemaphoreType.DMA,
            pltpu.SemaphoreType.DMA,
            pltpu.SemaphoreType.DMA,
            pltpu.SemaphoreType.DMA,
            pltpu.SemaphoreType.DMA((PHASES,)),
            pltpu.SemaphoreType.DMA((PHASES,)),
            pltpu.SemaphoreType.DMA((PHASES,)),
            pltpu.SemaphoreType.DMA,
            pltpu.SemaphoreType.DMA,
            pltpu.SemaphoreType.DMA,
            pltpu.SemaphoreType.DMA,
        ],
        compiler_params=pltpu.CompilerParams(
            collective_id=0, has_side_effects=True, vmem_limit_bytes=56 << 20
        ),
        cost_estimate=pl.CostEstimate(
            flops=2 * (2048 * 3072 + 2048 * 1024) * WIDTH, bytes_accessed=2 << 20, transcendentals=ROWS
        ),
    )(embeddings, cluster_ids.reshape(1, ROWS))
    return (out[0].reshape(ROWS), out[1].reshape(ROWS))


def solution(mesh):
    placed = (P(("files", "clus"), None), P(("files", "clus"), None))
    return jax.shard_map(
        body,
        mesh=mesh,
        in_specs=placed,
        out_specs=(P(("files", "clus")), P(("files", "clus"))),
        check_vma=False,
    )
```

time: 247 us -> 51.7 us (0.21)
  blocking collectives: 73.3 us -> 0 us
  waiting for transfers between devices: 67.7 us -> 0 us
  Pallas kernels: 0 us -> 49.3 us
  local copies, waits for them, and re-layouts: 35.8 us -> 1.28 us
  other arithmetic: 26.8 us -> 0 us
  matrix products: 16.4 us -> 0 us
  between operations: 14.2 us -> 0.64 us
  starting transfers between devices: 12.6 us -> 0 us
    all_to_all x2 -> x0, blocking collectives: 59.3 us -> none  [the longest x1 42 us: body(): lax.all_to_all(outgoing, ('files', 'clus'), split_axis=0, concat_axis=2,...]
    pallas_call x0 -> x1, Pallas kernels: none -> 49.3 us  [body(): pl.pallas_call(kernel, out_shape=jax.ShapeDtypeStruct((2, ROWS // LANES,...]
    all_gather x1 -> x0, waiting for transfers between devices: 47.8 us -> none  [body(): lax.all_gather(blocks, 'clus', axis=1, tiled=True)]
    gather x2 -> x0, local copies, waits for them, and re-layouts: 21.1 us -> none  [the longest x1 10.5 us: body(): earlier_best = returned_first.reshape(-1)[flat]]
    all_to_all x2 -> x0, waiting for transfers between devices: 19.8 us -> none  [the longest x1 10.2 us: body(): lax.all_to_all(first_best[None], ('files', 'clus'), split_axis=2, concat_...]
    another operation x5 -> x0, other arithmetic: 18.2 us -> none
    dot_general x1 -> x0, matrix products: 16.4 us -> none  [tile_maxima(): jnp.einsum('qmd,qnd->qmn', own, other, preferred_element_type=jnp.float32)]
    all_gather x1 -> x0, blocking collectives: 14.1 us -> none  [body(): lax.all_gather(block_ids, 'clus', axis=1, tiled=True)]
  transfers between devices with their start and end apart: 3 -> 0, of which waited for: 3 -> 0; matrix products, arithmetic and copies ran while one was open for 3% -> 0% of each run, Pallas kernels for 0% -> 0%
where the time goes in v2:
time: 51.7 us; the launch traced here: 51.3 us
  Pallas kernels  49.3 us (95%)
  local copies, waits for them, and re-layouts  1.28 us (2%)
  between operations  0.64 us (1%)
    pallas_call x1, Pallas kernels, body(): pl.pallas_call(kernel, out_shape=jax.ShapeDtypeStruct((2, ROWS // LANES,...  49.3 us
    another operation x1, local copies, waits for them, and re-layouts, body(): return (out[0].reshape(ROWS), out[1].reshape(ROWS))  1.28 us

profile of v2, /device:TPU:1, one launch (start us, length us, event | category | flops | bytes accessed | tf_op | source)
XLA Modules:
  0.0 51.3 jit_solution(7677346186200991887)
XLA Ops:
  0.6 49.3 %shard_map.41 = f32[2,8,128]{2,1,0:T(8,128)} custom-call(bf16[1024,512]{1,0:T(8,128)(2,1)} %emb_ref.1, s32[1,1024]{1,0:T(1,128)} %bitcast.5), custom_call_target="tpu_custom_call" | custom-call | flops 8589934592 | bytes 2097152 | tf_op jit(solution)/shard_map/pallas_call | solution.py:333
  50.0 1.3 %slice_bitcast_fusion = (f32[1024]{0:T(1024)}, f32[1024]{0:T(1024)}) fusion(f32[2,8,128]{2,1,0:T(8,128)} %shard_map.41), kind=kLoop, calls=%fused_computation | loop fusion | bytes 16384 | tf_op jit(solution)/shard_map/reshape;squeeze | solution.py:377

commit v3 on v2

--- a/solution.py
+++ b/solution.py
@@ -25,12 +25,18 @@
 NT = (((1,), (1,)), ((), ()))
 
 
+def hops(offset):
+    return sum(min(d, 4 - d) for d in offset)
+
+
+FAR_FIRST = [sorted(range(PER), key=lambda j: -hops(offsets(t, j))) for t in range(PHASES)]
+
+
 def kernel(
     emb_ref, lab_ref, out_ref,
     raw, lab, unit, outgoing, own, other, acc, cacc, bias_l, bias_s, masks, orders, res, ret, turned,
     onehot, rank_s, key_s, count_s,
     raw_sem, lab_sem, self_sem, send_sem, recv_sem, fwd_send, fwd_recv, ret_send, ret_recv,
-    ring_send, ring_recv,
 ):
     load = pltpu.make_async_copy(emb_ref, raw, raw_sem)
     load.start()
@@ -53,10 +59,10 @@
         return (zs[dz] * 4 + ys[dy], xs[dx] * 2 + core)
 
     barrier = pltpu.get_barrier_semaphore()
-    for t in range(PHASES):
-        for j in range(PER):
-            to = target(t, j) if t or j else partner
-            pl.semaphore_signal(barrier, inc=1, device_id=to, device_id_type=MESH)
+    everyone = [(t, j) for t in range(PHASES) for j in range(PER)]
+    for t, j in sorted(everyone, key=lambda tj: -hops(offsets(*tj))):
+        to = target(t, j) if t or j else partner
+        pl.semaphore_signal(barrier, inc=1, device_id=to, device_id_type=MESH)
 
     cluster = lax.broadcasted_iota(jnp.int32, (CHIPS, LANES), 0)
     blocks = ROWS // LANES
@@ -128,7 +134,7 @@
         if t == 0:
             pl.semaphore_wait(barrier, CHIPS)
             keep.start()
-        for j in range(PER):
+        for j in FAR_FIRST[t]:
             if t or j:
                 send(t, j).start()
 
@@ -250,40 +256,27 @@
     for i in range(16):
         for after in range(2):
             res[i, after : after + 1, :] = pltpu.roll(lines[i, after], x * CAP, 1)
-        if i:
-            give = pltpu.make_async_remote_copy(
-                src_ref=res.at[i],
-                dst_ref=ret.at[here],
-                send_sem=ret_send,
-                recv_sem=ret_recv,
-                device_id=(zs[-(i // 4) % 4] * 4 + ys[-(i % 4) % 4], clus),
-                device_id_type=MESH,
-            )
-            give.start()
-    ret[here] = res[0]
-
-    def tally(first, number, send_sem, recv_sem):
-        return pltpu.make_async_remote_copy(
-            src_ref=ret.at[pl.ds(first, number)],
-            dst_ref=ret.at[pl.ds(first, number)],
-            send_sem=send_sem,
-            recv_sem=recv_sem,
-            device_id=partner,
-            device_id_type=MESH,
-        )
-
-    tally(0, 15, ret_send, ret_recv).wait_recv()
-    column = ret.at[pl.ds(pl.multiple_of(x * 16, 16), 16)]
-    for d in range(1, 4):
+    back = [(dz, dy, dx) for dz in range(4) for dy in range(4) for dx in range(4)]
+    for dz, dy, dx in sorted(back, key=hops, reverse=True)[:-1]:
         pltpu.make_async_remote_copy(
-            src_ref=column,
-            dst_ref=column,
-            send_sem=ring_send,
-            recv_sem=ring_recv,
-            device_id=(files, xs[d] * 2 + core),
+            src_ref=res.at[dz * 4 + dy],
+            dst_ref=ret.at[here],
+            send_sem=ret_send,
+            recv_sem=ret_recv,
+            device_id=(zs[-dz % 4] * 4 + ys[-dy % 4], xs[-dx % 4] * 2 + core),
             device_id_type=MESH,
         ).start()
-    tally(0, 48, ring_send, ring_recv).wait_recv()
+    ret[here] = res[0]
+
+    returned = pltpu.make_async_remote_copy(
+        src_ref=ret.at[pl.ds(0, CHIPS - 1)],
+        dst_ref=ret.at[pl.ds(0, CHIPS - 1)],
+        send_sem=ret_send,
+        recv_sem=ret_recv,
+        device_id=partner,
+        device_id_type=MESH,
+    )
+    returned.wait_recv()
 
     for after in range(2):
         turned[after] = jnp.transpose(ret[:, after, :])
@@ -305,8 +298,7 @@
         for b in range(blocks):
             out_ref[after, b : b + 1, :] = value[:, b * LANES : (b + 1) * LANES]
 
-    tally(0, 15, ret_send, ret_recv).wait_send()
-    tally(0, 48, ring_send, ring_recv).wait_send()
+    returned.wait_send()
     sent = pltpu.make_async_remote_copy(
         src_ref=outgoing.at[0, pl.ds(0, PER - 1)],
         dst_ref=outgoing.at[0, pl.ds(0, PER - 1)],
@@ -326,6 +318,11 @@
     ).wait_send()
     for t in range(PHASES):
         forward(t).wait_send()
+
+
+def part(both_ref, first_ref, second_ref):
+    first_ref[...] = both_ref[0]
+    second_ref[...] = both_ref[1]
 
 
 def body(embeddings, cluster_ids):
@@ -364,8 +361,6 @@
             pltpu.SemaphoreType.DMA((PHASES,)),
             pltpu.SemaphoreType.DMA,
             pltpu.SemaphoreType.DMA,
-            pltpu.SemaphoreType.DMA,
-            pltpu.SemaphoreType.DMA,
         ],
         compiler_params=pltpu.CompilerParams(
             collective_id=0, has_side_effects=True, vmem_limit_bytes=56 << 20
@@ -374,7 +369,14 @@
             flops=2 * (2048 * 3072 + 2048 * 1024) * WIDTH, bytes_accessed=2 << 20, transcendentals=ROWS
         ),
     )(embeddings, cluster_ids.reshape(1, ROWS))
-    return (out[0].reshape(ROWS), out[1].reshape(ROWS))
+    line = jax.ShapeDtypeStruct((ROWS // LANES, LANES), jnp.float32)
+    first, second = pl.pallas_call(
+        part,
+        out_shape=(line, line),
+        in_specs=[pl.BlockSpec(memory_space=pltpu.VMEM)],
+        out_specs=[pl.BlockSpec(memory_space=pltpu.VMEM)] * 2,
+    )(out)
+    return (first.reshape(ROWS), second.reshape(ROWS))
 
 
 def solution(mesh):

time: 51.7 us -> 49.1 us (0.950)
  local copies, waits for them, and re-layouts: 1.28 us -> 0 us
  Pallas kernels: 49.3 us -> 48.3 us
    pallas_call x1, Pallas kernels: 49.3 us -> 47 us  [body(): pl.pallas_call(kernel, out_shape=jax.ShapeDtypeStruct((2, ROWS // LANES,...]
    pallas_call x0 -> x1, Pallas kernels: none -> 1.3 us  [body(): pl.pallas_call(part, out_shape=(line, line), in_specs=[pl.BlockSpec(memor...]
    another operation x1 -> x0, local copies, waits for them, and re-layouts: 1.28 us -> none  [body(): return (out[0].reshape(ROWS), out[1].reshape(ROWS))]
where the time goes in v3:
time: 49.1 us; the launch traced here: 49 us
  Pallas kernels  48.3 us (98%)
  between operations  0.64 us (1%)
    pallas_call x1, Pallas kernels, body(): pl.pallas_call(kernel, out_shape=jax.ShapeDtypeStruct((2, ROWS // LANES,...  47 us
    pallas_call x1, Pallas kernels, body(): pl.pallas_call(part, out_shape=(line, line), in_specs=[pl.BlockSpec(memor...  1.3 us

profile of v3, /device:TPU:1, one launch (start us, length us, event | category | flops | bytes accessed | tf_op | source)
XLA Modules:
  0.0 49.0 jit_solution(9621373481368875245)
XLA Ops:
  0.6 47.0 %shard_map.41.both_ref = f32[2,8,128]{2,1,0:T(8,128)} custom-call(bf16[1024,512]{1,0:T(8,128)(2,1)} %emb_ref.1, s32[1,1024]{1,0:T(1,128)} %bitcast.3), custom_call_target="tpu_custom_call" | custom-call | flops 8589934592 | bytes 2097152 | tf_op jit(solution)/shard_map/pallas_call | solution.py:330
  47.7 1.3 %shard_map.42 = (f32[8,128]{1,0:T(8,128)}, f32[8,128]{1,0:T(8,128)}) custom-call(f32[2,8,128]{2,1,0:T(8,128)} %shard_map.41.both_ref), custom_call_target="tpu_custom_call" | custom-call | tf_op jit(solution)/shard_map/pallas_call | solution.py:373

commit v4 on v3

--- a/solution.py
+++ b/solution.py
@@ -329,7 +329,7 @@
     anywhere = pl.BlockSpec(memory_space=pl.ANY)
     out = pl.pallas_call(
         kernel,
-        out_shape=jax.ShapeDtypeStruct((2, ROWS // LANES, LANES), jnp.float32),
+        out_shape=pltpu.VMEM((2, ROWS // LANES, LANES), jnp.float32),
         in_specs=[anywhere, anywhere],
         out_specs=pl.BlockSpec(memory_space=pltpu.VMEM),
         scratch_shapes=[
@@ -375,7 +375,7 @@
         out_shape=(line, line),
         in_specs=[pl.BlockSpec(memory_space=pltpu.VMEM)],
         out_specs=[pl.BlockSpec(memory_space=pltpu.VMEM)] * 2,
-    )(out)
+    )(pltpu.with_memory_space_constraint(out, pltpu.VMEM))
     return (first.reshape(ROWS), second.reshape(ROWS))
 
 

time: 49.1 us -> 47.8 us (0.974)
  Pallas kernels: 48.3 us -> 47 us
    pallas_call x1, Pallas kernels: 1.3 us -> 0.6 us  [body(): pl.pallas_call(part, out_shape=(line, line), in_specs=[pl.BlockSpec(memor...]
    pallas_call x1, Pallas kernels: 47 us -> 46.4 us  [body(): pl.pallas_call(kernel, out_shape=pltpu.VMEM((2, ROWS // LANES, LANES), jn...]
where the time goes in v4:
time: 47.8 us; the launch traced here: 47.7 us
  Pallas kernels  47 us (98%)
  between operations  0.64 us (1%)
    pallas_call x1, Pallas kernels, body(): pl.pallas_call(kernel, out_shape=pltpu.VMEM((2, ROWS // LANES, LANES), jn...  46.4 us

profile of v4, /device:TPU:1, one launch (start us, length us, event | category | flops | bytes accessed | tf_op | source)
XLA Modules:
  0.0 47.7 jit_solution(6225674362489918251)
XLA Ops:
  0.6 46.4 %shard_map.41.both_ref = f32[2,8,128]{2,1,0:T(8,128)S(1)} custom-call(bf16[1024,512]{1,0:T(8,128)(2,1)} %emb_ref.1, s32[1,1024]{1,0:T(1,128)} %bitcast.3), custom_call_target="tpu_custom_call" | custom-call | flops 8589934592 | bytes 2097152 | tf_op jit(solution)/shard_map/pallas_call | solution.py:330
  47.1 0.6 %shard_map.42 = (f32[8,128]{1,0:T(8,128)}, f32[8,128]{1,0:T(8,128)}) custom-call(f32[2,8,128]{2,1,0:T(8,128)S(1)} %shard_map.41.both_ref), custom_call_target="tpu_custom_call" | custom-call | tf_op jit(solution)/shard_map/pallas_call | solution.py:373

commit v5 on v4

--- a/solution.py
+++ b/solution.py
@@ -16,9 +16,13 @@
 BLOCK = PER * CAP
 
 
+COSETS = (0, 7, 6, 5, 4, 3, 2, 1)
+
+
 def offsets(t, j):
     a = -j % 4
-    return (a + t % 4) % 4, (a + 2 * (j // 4) + t // 4) % 4, a
+    coset = COSETS[t]
+    return (a + coset % 4) % 4, (a + 2 * (j // 4) + coset // 4) % 4, a
 
 
 EMPTY = 2.0
@@ -138,14 +142,15 @@
             if t or j:
                 send(t, j).start()
 
-    def chip_order(t, j):
+    def chip_order(coset, j):
         a = -j % 4
-        sz = (z - a - t % 4) % 4
-        sy = (y - a - 2 * (j // 4) - t // 4) % 4
+        sz = (z - a - coset % 4) % 4
+        sy = (y - a - 2 * (j // 4) - coset // 4) % 4
         return sz * 16 + sy * 4 + (x + j) % 4
 
-    i = lax.broadcasted_iota(jnp.int32, (CHIPS, LANES), 0)
-    orders[...] = chip_order(i // PER, i % PER)
+    i = lax.broadcasted_iota(jnp.int32, (PER, LANES), 0)
+    for t in range(PHASES):
+        orders[t * PER : (t + 1) * PER, :] = chip_order(COSETS[t], i)
     lane_j = lax.broadcasted_iota(jnp.int32, (1, BLOCK), 1) // CAP
     row_i = lax.broadcasted_iota(jnp.int32, (BLOCK, LANES), 0)
 
@@ -162,7 +167,7 @@
         bias_l[t * 2 + side] = jnp.transpose(mark)[0:1, :]
 
         if t:
-            columns = chip_order(t, lane_j)
+            columns = chip_order(COSETS[t], lane_j)
             rows = orders[: t * PER, 0:1]
             masks[side, 0, : t * PER, :] = jnp.where(columns < rows, bias_l[t * 2 + side], -4.0)
             masks[side, 1, : t * PER, :] = jnp.where(columns > rows, bias_l[t * 2 + side], -4.0)
@@ -189,8 +194,8 @@
         similar = product(rows_of(own, t, t + 1), rows_of(other if side else own, t, t + 1))
         similar = similar + bias_l[t * 2 + side]
         lane = lax.broadcasted_iota(jnp.int32, (1, BLOCK), 1)
-        mine = (chip_order(t, row_i // CAP) * (2 * CAP) + row_i % CAP)[:, 0:1]
-        theirs = chip_order(t, lane_j) * (2 * CAP) + lane % CAP
+        mine = (chip_order(COSETS[t], row_i // CAP) * (2 * CAP) + row_i % CAP)[:, 0:1]
+        theirs = chip_order(COSETS[t], lane_j) * (2 * CAP) + lane % CAP
         if side:
             theirs = theirs + (1 - 2 * core) * CAP
         for after in range(2):

time: 47.8 us -> 47.6 us (level)
  no operation moved by 1% of the time
where the time goes in v5:
time: 47.6 us; the launch traced here: 47.5 us
  Pallas kernels  46.8 us (98%)
  between operations  0.64 us (1%)
    pallas_call x1, Pallas kernels, body(): pl.pallas_call(kernel, out_shape=pltpu.VMEM((2, ROWS // LANES, LANES), jn...  46.2 us

profile of v5, /device:TPU:1, one launch (start us, length us, event | category | flops | bytes accessed | tf_op | source)
XLA Modules:
  0.0 47.5 jit_solution(13952318894101613032)
XLA Ops:
  0.6 46.2 %shard_map.41.both_ref = f32[2,8,128]{2,1,0:T(8,128)S(1)} custom-call(bf16[1024,512]{1,0:T(8,128)(2,1)} %emb_ref.1, s32[1,1024]{1,0:T(1,128)} %bitcast.3), custom_call_target="tpu_custom_call" | custom-call | flops 8589934592 | bytes 2097152 | tf_op jit(solution)/shard_map/pallas_call | solution.py:335
  46.9 0.6 %shard_map.42 = (f32[8,128]{1,0:T(8,128)}, f32[8,128]{1,0:T(8,128)}) custom-call(f32[2,8,128]{2,1,0:T(8,128)S(1)} %shard_map.41.both_ref), custom_call_target="tpu_custom_call" | custom-call | tf_op jit(solution)/shard_map/pallas_call | solution.py:378

commit v6 on v5

--- a/solution.py
+++ b/solution.py
@@ -247,24 +247,18 @@
             maxima(product(rows_of(own, 0, t), rows_of(other, t, t + 1)), t, 1, 0, True, None)
         diagonal(t, 1)
 
-    quarter = lax.broadcasted_iota(jnp.int32, (1, LANES), 1) // CAP
-    lines = {}
     for t in range(PHASES):
         for after in range(2):
             best = jnp.max(jnp.transpose(acc[after, t]), axis=0, keepdims=True)
             best = jnp.maximum(best, jnp.max(cacc[t, after], axis=0, keepdims=True))
-            for j in range(PER):
-                dz, dy, dx = offsets(t, j)
-                line = best[:, j // 4 * LANES : (j // 4 + 1) * LANES]
-                key = (dz * 4 + dy, after)
-                lines[key] = jnp.where(quarter == j % 4, line, lines[key]) if key in lines else line
-    for i in range(16):
-        for after in range(2):
-            res[i, after : after + 1, :] = pltpu.roll(lines[i, after], x * CAP, 1)
+            for half in range(2):
+                line = best[:, half * LANES : (half + 1) * LANES]
+                res[t * 2 + half, after : after + 1, :] = pltpu.roll(line, x * CAP, 1)
+    line_of = {offsets(t, j): t * 2 + j // 4 for t in range(PHASES) for j in range(PER)}
     back = [(dz, dy, dx) for dz in range(4) for dy in range(4) for dx in range(4)]
     for dz, dy, dx in sorted(back, key=hops, reverse=True)[:-1]:
         pltpu.make_async_remote_copy(
-            src_ref=res.at[dz * 4 + dy],
+            src_ref=res.at[line_of[dz, dy, dx]],
             dst_ref=ret.at[here],
             send_sem=ret_send,
             recv_sem=ret_recv,

time: 47.6 us -> 47.7 us (level)
  no operation moved by 1% of the time
where the time goes in v6:
time: 47.7 us; the launch traced here: 47.5 us
  Pallas kernels  46.9 us (98%)
  between operations  0.64 us (1%)
    pallas_call x1, Pallas kernels, body(): pl.pallas_call(kernel, out_shape=pltpu.VMEM((2, ROWS // LANES, LANES), jn...  46.3 us

profile of v6, /device:TPU:1, one launch (start us, length us, event | category | flops | bytes accessed | tf_op | source)
XLA Modules:
  0.0 47.5 jit_solution(14578533201478794389)
XLA Ops:
  0.6 46.3 %shard_map.41.both_ref = f32[2,8,128]{2,1,0:T(8,128)S(1)} custom-call(bf16[1024,512]{1,0:T(8,128)(2,1)} %emb_ref.1, s32[1,1024]{1,0:T(1,128)} %bitcast.3), custom_call_target="tpu_custom_call" | custom-call | flops 8589934592 | bytes 2097152 | tf_op jit(solution)/shard_map/pallas_call | solution.py:329
  46.9 0.6 %shard_map.42 = (f32[8,128]{1,0:T(8,128)}, f32[8,128]{1,0:T(8,128)}) custom-call(f32[2,8,128]{2,1,0:T(8,128)S(1)} %shard_map.41.both_ref), custom_call_target="tpu_custom_call" | custom-call | tf_op jit(solution)/shard_map/pallas_call | solution.py:372

commit v7 on v6

--- a/solution.py
+++ b/solution.py
@@ -230,8 +230,8 @@
     for t in range(PHASES):
         if t == 0:
             keep.wait()
-        arrived(t)
-        forward(t).start()
+            arrived(0)
+            forward(0).start()
         set_bias(own, t, 0)
         mine = rows_of(own, t, t + 1)
         best = [jnp.full((8, BLOCK), -1.0, jnp.float32)] * 2
@@ -242,6 +242,9 @@
             cacc[t, after] = best[after]
         diagonal(t, 0)
         forward(t).wait_recv()
+        if t + 1 < PHASES:
+            arrived(t + 1)
+            forward(t + 1).start()
         set_bias(other, t, 1)
         if t:
             maxima(product(rows_of(own, 0, t), rows_of(other, t, t + 1)), t, 1, 0, True, None)

time: 47.7 us -> 47.7 us (level)
  no operation moved by 1% of the time
where the time goes in v7:
time: 47.7 us; the launch traced here: 47.3 us
  Pallas kernels  46.6 us (98%)
  between operations  0.64 us (1%)
    pallas_call x1, Pallas kernels, body(): pl.pallas_call(kernel, out_shape=pltpu.VMEM((2, ROWS // LANES, LANES), jn...  46 us

profile of v7, /device:TPU:1, one launch (start us, length us, event | category | flops | bytes accessed | tf_op | source)
XLA Modules:
  0.0 47.3 jit_solution(4623411506447228023)
XLA Ops:
  0.6 46.0 %shard_map.41.both_ref = f32[2,8,128]{2,1,0:T(8,128)S(1)} custom-call(bf16[1024,512]{1,0:T(8,128)(2,1)} %emb_ref.1, s32[1,1024]{1,0:T(1,128)} %bitcast.3), custom_call_target="tpu_custom_call" | custom-call | flops 8589934592 | bytes 2097152 | tf_op jit(solution)/shard_map/pallas_call | solution.py:332
  46.7 0.6 %shard_map.42 = (f32[8,128]{1,0:T(8,128)}, f32[8,128]{1,0:T(8,128)}) custom-call(f32[2,8,128]{2,1,0:T(8,128)S(1)} %shard_map.41.both_ref), custom_call_target="tpu_custom_call" | custom-call | tf_op jit(solution)/shard_map/pallas_call | solution.py:375
